TPU v7x, 128 devices: a whole 4x4x4 slice. The times are simulated.
128 devices in a mesh: sensor: 16 (over z, x), partner: 8 (over y, core).
Axes of the slice: x: 4, y: 4, z: 4, core: 2. Of those that a mesh axis runs over, the one named last changes fastest.
Arguments:
- spectra: bfloat16 [2048, 3, 2, 512], P(('sensor', 'partner')), may hold values from -6 to 6
- pair_slot: int32 [2048, 128], P(('sensor', 'partner')), may hold values from 0 to 255, as said below
- slot_cell: int32 [16, 256], replicated, may hold values from -1 to 4095, as said below
- cell_rank: int32 [4096], replicated, may hold values from 0 to 4095, as said below
Outputs:
- correlations: bfloat16 [4096, 9, 1024], P(('sensor', 'partner'))
Inputs may be any that keep to these rules, and one draw needn't show every extreme that they name: `cell_rank`: A permutation of the cell numbers; the device of mesh index d (sensor index times 8 plus partner index) owns the cells of rank d * 32 to (d + 1) * 32 - 1. `slot_cell`: row g holds the cells of sensor group g's slots in blocks of 2 per device in mesh order; every cell in device d's block is owned by device d; -1 marks an unused slot; cells in one block are distinct and unused slots come last in it; in every draw some device's block is full in every row. `pair_slot`: entry [i, j] is the slot, in the row of sensor i's group, that takes the pair of sensor i and the j-th sensor of its group; it never names an unused slot.
All inputs are finite; a program needn't handle non-finite values.
Results may differ from a plain program's by a relative error of at most 0.011.
Values may be sent and summed in bfloat16 or wider, within the bound.
A program may use at most 128 MiB of HBM per device.

v0:
```python
import math

import jax
import jax.numpy as jnp
from jax import lax
from jax.sharding import PartitionSpec as P


def cross_spectra(resident, partners):
    res_real = resident[:, :, 0, :].astype(jnp.float32)
    res_imag = resident[:, :, 1, :].astype(jnp.float32)
    par_real = partners[:, :, 0, :].astype(jnp.float32)
    par_imag = partners[:, :, 1, :].astype(jnp.float32)
    left_real = res_real[:, None, :, None, :]
    left_imag = res_imag[:, None, :, None, :]
    right_real = par_real[None, :, None, :, :]
    right_imag = par_imag[None, :, None, :, :]
    real_part = left_real * right_real + left_imag * right_imag
    imag_part = left_imag * right_real - left_real * right_imag
    joined = jnp.stack([real_part, imag_part], axis=4)
    return joined.reshape(resident.shape[0] * partners.shape[0], -1).astype(jnp.bfloat16)


def lag_table(freqs, lags):
    bins = jnp.arange(freqs, dtype=jnp.int32)[:, None]
    shifts = jnp.arange(lags, dtype=jnp.int32)[None, :] - lags // 2
    phase = jnp.mod(bins * shifts, lags).astype(jnp.float32)
    angle = phase * (2.0 * math.pi / lags)
    return jnp.concatenate([jnp.cos(angle), -jnp.sin(angle)], axis=0) / freqs


def on_device(spectra, pair_slot, slot_cell, cell_rank):
    resident_count = spectra.shape[0]
    freqs = spectra.shape[3]
    width = 18 * freqs
    slot_count = slot_cell.shape[1]
    groups_count = lax.axis_size("sensor")
    blocks_count = lax.axis_size("partner")
    devices_count = groups_count * blocks_count
    capacity = slot_count // devices_count
    cells_dev = cell_rank.shape[0] // devices_count
    slot_ids = jnp.arange(slot_count, dtype=jnp.int32)
    piece = lax.all_gather(spectra, "partner", axis=0, tiled=True)
    piece_rows = piece.shape[0]
    step_rows = math.gcd(resident_count, max(1, 1024 // piece_rows))

    def add_block(index, carried):
        first = index * step_rows
        resident = lax.dynamic_slice_in_dim(spectra, first, step_rows, 0)
        slots = lax.dynamic_slice_in_dim(pair_slot, first, step_rows, 0).reshape(-1)
        products = cross_spectra(resident, piece)
        selector = (slots[:, None] == slot_ids[None, :]).astype(jnp.bfloat16)
        return carried + jnp.einsum(
            "ps,px->sx", selector, products, preferred_element_type=jnp.float32
        )

    partial_value = lax.fori_loop(
        0, resident_count // step_rows, add_block, jnp.zeros((slot_count, width), jnp.float32)
    )
    device_index = lax.axis_index(("sensor", "partner"))
    my_cells = lax.dynamic_slice_in_dim(slot_cell, device_index * capacity, capacity, 1)
    ranks = jnp.take(cell_rank, jnp.maximum(my_cells, 0))
    local = jnp.where(my_cells >= 0, ranks - device_index * cells_dev, -1)
    matches = local[:, :, None] == jnp.arange(cells_dev, dtype=jnp.int32)[None, None, :]
    moved = lax.all_to_all(
        partial_value.astype(jnp.bfloat16),
        ("sensor", "partner"),
        split_axis=0,
        concat_axis=0,
        tiled=True,
    )
    moved = moved.reshape(groups_count, blocks_count, capacity, width)
    stacked = jnp.einsum(
        "gkc,gqkx->cx", matches.astype(jnp.bfloat16), moved, preferred_element_type=jnp.float32
    )
    table = lag_table(freqs, 2 * freqs)
    shaped = stacked.reshape(cells_dev, 9, 2 * freqs)
    result = jnp.einsum("cax,xt->cat", shaped, table, precision=lax.Precision.HIGHEST)
    return result.astype(jnp.bfloat16)


def solution(mesh):
    in_specs = (
        P(("sensor", "partner"), None, None, None),
        P(("sensor", "partner"), None),
        P(),
        P(),
    )
    out_specs = P(("sensor", "partner"), None, None)
    return jax.shard_map(
        on_device, mesh=mesh, in_specs=in_specs, out_specs=out_specs, check_vma=False
    )
```

profile of v0, /device:TPU:1, one launch (start us, length us, event | category | flops | bytes accessed | tf_op | source)
XLA Modules:
  0.0 259.4 jit_solution(10807884469015256612)
XLA Ops:
  0.0 0.0 copy-start
  0.0 0.9 copy.32
  0.9 15.2 %all_gather.3 = bf16[128,3,2,512]{3,0,2,1:T(8,128)(2,1)S(1)} all-gather(bf16[16,3,2,512]{3,0,2,1:T(8,128)(2,1)S(1)} %copy.32), channel_id=1, replica_groups=mesh['sensor'=16,'partner'=8] {'partner'}, dimensions={0}, use_global_device_ids=true | all-gather | bytes 884736 | tf_op jit(solution)/shard_map/all_gather | solution.py:43
  16.2 145.2 %while.14 = (s32[]{:T(128)}, f32[256,9216]{1,0:T(8,128)}, s32[16,128]{1,0:T(8,128)}, bf16[16,3,2,512]{3,0,2,1:T(8,128)(2,1)S(1)}, bf16[128,3,2,512]{3,0,2,1:T(8,...) while((s32[]{:T(128)}, f32[256,9216]{1,0:T(8,128)}, ...), condition=%wide.region_1.0_spmd.clone, body=%wide.region_0.0_spmd.clone.sunk | while | flops 4884684800 | bytes 136540384 | solution.py:57
  16.2 0.2 bitcast_convert_fusion.3
  16.5 12.1 %add_convert_fusion.2 = (bf16[8,128,3,3,1,512]{5,1,4,3,2,0:T(8,128)(2,1)}, bf16[8,128,3,3,1,512]{5,1,4,3,2,0:T(8,128)(2,1)}) fusion(f32[128,3,512]{2,0,1:T(8,128)S(1)} %get-tuple-element.210, f32[8,3,512]{2,1,0:T(4,128)S(1)} %copy.52, f32[128,3,512]{2,0,1:T(8,128)S(1)} %get-tuple-element.212, f32[8,3,512]{2,1,0:T(4,128)S(1)} %copy.53), kind=kLoop, calls=%fused_computation.7.clone.1 | loop fusion | flops 37748736 | bytes 20545536 | tf_op jit(solution)/shard_map/convert.4
  28.6 16.5 %pad_maximum_fusion.2 = bf16[8,128,3,3,2,512]{5,1,4,3,2,0:T(8,128)(2,1)} fusion(bf16[8,128,3,3,1,512]{5,1,4,3,2,0:T(8,128)(2,1)} %get-tuple-element.214, bf16[8,128,3,3,1,512]{5,1,4,3,2,0:T(8,128)(2,1)} %get-tuple-element.215), kind=kLoop, calls=%fused_computation.5.clone.1 | loop fusion | flops 9437184 | bytes 37748736 | tf_op jit(solution)/shard_map/while/body/eval_jaxpr/stack | solution.py:20
  45.1 0.0 copy-start.1
  45.1 26.1 %copy.54 = bf16[8,128,3,3,2,512]{1,0,5,4,3,2:T(8,128)(2,1)} copy(bf16[8,128,3,3,2,512]{5,1,4,3,2,0:T(8,128)(2,1)} %pad_maximum_fusion.2) | data formatting | bytes 37748736 | tf_op jit(solution)/shard_map/while/body/eval_jaxpr/stack | solution.py:20
  71.2 0.0 copy-done.1
  71.2 16.9 %fusion.43 = f32[256,9216]{1,0:T(8,128)} fusion(bf16[1152,8,8,128]{3,2,1,0:T(8,128)(2,1)} %bitcast.55, f32[256,9216]{1,0:T(8,128)} %get-tuple-element.227, pred[]{:T(512)S(6)} %compare.4, s32[1024]{0:T(1024)S(1)} %dynamic-slice_bitcast_fusion.4), kind=kOutput, calls=%fused_computation.8.clone.1 | convolution fusion | flops 4837081088 | bytes 37752832 | tf_op jit(solution)/shard_map/while/body/eval_jaxpr/ps,px->sx/dot_general | solution.py:53
  88.1 0.2 bitcast_convert_fusion.3
  88.5 12.1 %add_convert_fusion.2 = (bf16[8,128,3,3,1,512]{5,1,4,3,2,0:T(8,128)(2,1)}, bf16[8,128,3,3,1,512]{5,1,4,3,2,0:T(8,128)(2,1)}) fusion(f32[128,3,512]{2,0,1:T(8,128)S(1)} %get-tuple-element.210, f32[8,3,512]{2,1,0:T(4,128)S(1)} %copy.52, f32[128,3,512]{2,0,1:T(8,128)S(1)} %get-tuple-element.212, f32[8,3,512]{2,1,0:T(4,128)S(1)} %copy.53), kind=kLoop, calls=%fused_computation.7.clone.1 | loop fusion | flops 37748736 | bytes 20545536 | tf_op jit(solution)/shard_map/convert.4
  100.5 16.5 %pad_maximum_fusion.2 = bf16[8,128,3,3,2,512]{5,1,4,3,2,0:T(8,128)(2,1)} fusion(bf16[8,128,3,3,1,512]{5,1,4,3,2,0:T(8,128)(2,1)} %get-tuple-element.214, bf16[8,128,3,3,1,512]{5,1,4,3,2,0:T(8,128)(2,1)} %get-tuple-element.215), kind=kLoop, calls=%fused_computation.5.clone.1 | loop fusion | flops 9437184 | bytes 37748736 | tf_op jit(solution)/shard_map/while/body/eval_jaxpr/stack | solution.py:20
  117.1 0.0 copy-start.1
  117.1 26.1 %copy.54 = bf16[8,128,3,3,2,512]{1,0,5,4,3,2:T(8,128)(2,1)} copy(bf16[8,128,3,3,2,512]{5,1,4,3,2,0:T(8,128)(2,1)} %pad_maximum_fusion.2) | data formatting | bytes 37748736 | tf_op jit(solution)/shard_map/while/body/eval_jaxpr/stack | solution.py:20
  143.2 0.0 copy-done.1
  143.2 18.2 %fusion.43 = f32[256,9216]{1,0:T(8,128)} fusion(bf16[1152,8,8,128]{3,2,1,0:T(8,128)(2,1)} %bitcast.55, f32[256,9216]{1,0:T(8,128)} %get-tuple-element.227, pred[]{:T(512)S(6)} %compare.4, s32[1024]{0:T(1024)S(1)} %dynamic-slice_bitcast_fusion.4), kind=kOutput, calls=%fused_computation.8.clone.1 | convolution fusion | flops 4837081088 | bytes 37752832 | tf_op jit(solution)/shard_map/while/body/eval_jaxpr/ps,px->sx/dot_general | solution.py:53
  161.4 6.5 %convert_element_type.85 = bf16[256,9216]{1,0:T(8,128)(2,1)} convert(f32[256,9216]{1,0:T(8,128)} %get-tuple-element.114) | non-fusion elementwise | flops 2359296 | bytes 14155776 | tf_op jit(solution)/shard_map/convert_element_type | solution.py:66
  167.9 7.5 %all_to_all.6 = bf16[128,2,9216]{2,1,0:T(2,128)(2,1)} reshape(bf16[256,9216]{1,0:T(8,128)(2,1)} %convert_element_type.85) | data formatting | bytes 9437184 | tf_op jit(solution)/shard_map/all_to_all | solution.py:65
  175.4 0.0 copy-start.2
  175.4 9.9 %all-to-all-start = ((bf16[128,2,9216]{2,1,0:T(2,128)(2,1)}), bf16[128,2,9216]{2,1,0:T(2,128)(2,1)}, u32[]{:S(2)}, u32[]{:S(2)}) async-start(bf16[128,2,9216]{2,1,0:T(2,128)(2,1)} %all_to_all.6), calls=%async_computation | async-start | bytes 9437184 | tf_op jit(solution)/shard_map/all_to_all | solution.py:65
  185.4 0.0 copy-done.2
  185.4 0.1 dynamic-slice_maximum_fusion
  185.5 0.1 reshape.91
  185.6 0.0 copy-done
  185.6 0.7 gather_fusion
  186.3 0.1 reshape.90
  186.4 0.1 subtract_select_fusion
  186.5 0.1 copy.30
  186.5 9.3 %fusion.29 = (f32[512,1024]{1,0:T(8,128)}, f32[512,1024]{1,0:T(8,128)}) fusion(s32[1024]{0:T(1024)S(1)} %iota_add_fusion), kind=kLoop, calls=%fused_computation.39 | loop fusion | flops 7864320 | bytes 4198400 | tf_op jit(solution)/shard_map/cos | solution.py:29
  195.9 48.0 %all-to-all-done = bf16[128,2,9216]{2,1,0:T(2,128)(2,1)} async-done(((bf16[128,2,9216]{2,1,0:T(2,128)(2,1)}), bf16[128,2,9216]{2,1,0:T(2,128)(2,1)}, u32[]{:S(2)}, u32[]{:S(2)}) %all-to-all-start) | async-done | bytes 4718624 | tf_op jit(solution)/shard_map/all_to_all | solution.py:65
  243.9 7.1 %convert_reduce_fusion = bf16[16,2,9216]{2,1,0:T(2,128)(2,1)S(1)} fusion(bf16[128,2,9216]{2,1,0:T(2,128)(2,1)} %all-to-all-done), kind=kLoop, calls=%fused_computation.19 | loop fusion | flops 4423680 | bytes 5308416 | tf_op jit(solution)/shard_map/gkc,gqkx->cx/reduce_sum | solution.py:73
  251.0 0.4 reshape.106
  251.4 0.9 convolution_bitcast_fusion
  252.3 7.1 %fusion.25 = bf16[32,9,1024]{2,0,1:T(8,128)(2,1)} fusion(f32[32,9,1024]{2,0,1:T(8,128)S(1)} %convolution_bitcast_fusion, f32[512,1024]{1,0:T(8,128)} %get-tuple-element.172, f32[512,1024]{1,0:T(8,128)} %get-tuple-element.171), kind=kOutput, calls=%fused_computation.37 | convolution fusion | flops 3626270720 | bytes 5963776 | tf_op jit(solution)/shard_map/cax,xt->cat/dot_general | solution.py:78
  (11 shorter events, 0.2 us)
Async XLA Ops:
  0.0 185.6 %copy-start = (s32[4096]{0:T(1024)S(1)}, s32[4096]{0:T(1024)}, u32[]{:S(2)}) copy-start(s32[4096]{0:T(1024)} %param.9) | copy-start | bytes 49156
  45.1 26.1 %copy-start.1 = (s32[16,128]{1,0:T(8,128)S(1)}, s32[16,128]{1,0:T(8,128)}, u32[]{:S(2)}) copy-start(s32[16,128]{1,0:T(8,128)} %get-tuple-element.238) | copy-start | bytes 24580 | tf_op jit(solution)/shard_map/while
  117.1 26.1 %copy-start.1 = (s32[16,128]{1,0:T(8,128)S(1)}, s32[16,128]{1,0:T(8,128)}, u32[]{:S(2)}) copy-start(s32[16,128]{1,0:T(8,128)} %get-tuple-element.238) | copy-start | bytes 24580 | tf_op jit(solution)/shard_map/while
  175.4 10.0 %copy-start.2 = (s32[16,256]{1,0:T(8,128)S(1)}, s32[16,256]{1,0:T(8,128)}, u32[]{:S(2)}) copy-start(s32[16,256]{1,0:T(8,128)} %param.8) | copy-start | bytes 49156
  175.4 68.4 %all-to-all-start = ((bf16[128,2,9216]{2,1,0:T(2,128)(2,1)}), bf16[128,2,9216]{2,1,0:T(2,128)(2,1)}, u32[]{:S(2)}, u32[]{:S(2)}) async-start(bf16[128,2,9216]{2,1,0:T(2,128)(2,1)} %all_to_all.6), calls=%async_computation | async-start | bytes 9437184 | tf_op jit(solution)/shard_map/all_to_all | solution.py:65
where the time goes:
time: 261 us; the launch traced here: 259 us
  other arithmetic  80.8 us (31%)
  local copies, waits for them, and re-layouts  62.2 us (24%)
  waiting for transfers between devices  48 us (18%)
  matrix products  43.1 us (17%)
  blocking collectives  15.2 us (6%)
  starting transfers between devices  9.94 us (4%)
    another operation x2, local copies, waits for them, and re-layouts, cross_spectra(): joined = jnp.stack([real_part, imag_part], axis=4)  52.2 us
    all_to_all x1, waiting for transfers between devices, on_device(): lax.all_to_all(partial_value.astype(jnp.bfloat16), ('sensor', 'partner'),...  48 us
    dot_general x2, matrix products, add_block(): jnp.einsum('ps,px->sx', selector, products, preferred_element_type=jnp.fl...  35.2 us
    another operation x2, other arithmetic, cross_spectra(): joined = jnp.stack([real_part, imag_part], axis=4)  33.1 us
    another operation x2, other arithmetic  24.1 us
    all_gather x1, blocking collectives, on_device(): piece = lax.all_gather(spectra, 'partner', axis=0, tiled=True)  15.2 us
    all_to_all x1, starting transfers between devices, on_device(): lax.all_to_all(partial_value.astype(jnp.bfloat16), ('sensor', 'partner'),...  9.94 us
    cos x1, other arithmetic, lag_table(): return jnp.concatenate([jnp.cos(angle), -jnp.sin(angle)], axis=0) / freqs  9.32 us
  transfers between devices with their start and end apart: 1, of which 1 were waited for; matrix products, arithmetic and copies ran while one was open for 4% of the time, Pallas kernels for 0%

commit v1 on v0

v1 whole, which is shorter than its diff:
```python
import functools
import math

import jax
import jax.numpy as jnp
import numpy as np
from jax import lax
from jax.experimental import pallas as pl
from jax.experimental.pallas import tpu as pltpu
from jax.sharding import PartitionSpec as P

MESH = pl.DeviceIdType.MESH
CHUNKS = (((0, 1, 2, 3), 32), ((4, 5, 6, 7), 32), ((8,), 64))


def lag_table(freqs, blocks):
    lags = 2 * freqs
    bins = np.arange(freqs)[:, None]
    shifts = np.arange(lags)[None, :] - lags // 2
    angle = np.mod(bins * shifts, lags) * (2.0 * math.pi / lags)
    both = np.stack([np.cos(angle), -np.sin(angle)]) / freqs
    both = both.reshape(2, blocks, freqs // blocks, lags).transpose(1, 0, 2, 3)
    return both.reshape(2 * freqs, lags).astype(jnp.bfloat16)


def kernel(sizes, mine_ref, target_ref, table_hbm, out_ref, got, left, right_r, right_i, slots,
           selector, total, table, send_a, recv_a, send_b, recv_b, table_sem,
           x_send, x_recv, a_send, a_recv, b_send, b_recv):
    groups, blocks, rows, cells = sizes
    sensors = blocks * rows
    own_g, own_b = lax.axis_index("sensor"), lax.axis_index("partner")
    half = out_ref.shape[2] // blocks // 2

    table_copy = pltpu.make_async_copy(table_hbm, table, table_sem)
    table_copy.start()

    barrier = pltpu.get_barrier_semaphore()
    for step in range(1, blocks):
        pl.semaphore_signal(barrier, inc=1, device_id=(own_g, lax.rem(own_b + step, blocks)), device_id_type=MESH)
    for step in range(1, groups):
        pl.semaphore_signal(barrier, inc=1, device_id=(lax.rem(own_g + step, groups), own_b), device_id_type=MESH)
    pl.semaphore_wait(barrier, blocks + groups - 2)

    def bins_copy(step, source):
        to = lax.rem(own_b + step, blocks)
        return pltpu.make_async_remote_copy(
            src_ref=mine_ref.at[to], dst_ref=got.at[source], send_sem=x_send.at[step], recv_sem=x_recv.at[step],
            device_id=(own_g, to), device_id_type=MESH)

    for step in range(1, blocks):
        bins_copy(step, own_b).start()
    got[own_b] = mine_ref[own_b]
    for step in range(1, blocks):
        bins_copy(step, lax.rem(own_b - step + blocks, blocks)).wait_recv()

    low = lax.broadcasted_iota(jnp.int32, (sensors, 2 * half), 1) < half
    for a in range(3):
        x = got[:, a].reshape(sensors, 2 * half).astype(jnp.float32)
        swapped = pltpu.roll(x, half, 1)
        left[a] = x
        left[3 + a] = jnp.where(low, swapped, -swapped)
        right_r[a] = jnp.where(low, x, swapped).astype(jnp.bfloat16)
        right_i[a] = jnp.where(low, swapped, x).astype(jnp.bfloat16)
    slots[...] = got[:, 3].reshape(sensors, sensors).astype(jnp.float32)

    slot_count = selector.shape[0]
    ids = lax.broadcasted_iota(jnp.int32, (slot_count, sensors), 0).astype(jnp.float32).astype(jnp.bfloat16)

    def select(i, carried):
        row = jnp.broadcast_to(slots[pl.ds(i, 1), :], (16, sensors)).astype(jnp.bfloat16)
        row = jnp.concatenate([row] * (slot_count // 16), axis=0)
        columns = pl.ds(pl.multiple_of(i * sensors, sensors), sensors)
        selector[:, columns] = jnp.where(row == ids, jnp.bfloat16(1), jnp.bfloat16(0))
        return carried

    lax.fori_loop(0, sensors, select, 0)

    def slot_sums(chunk, per_step, width):
        def add(step, carried):
            blocks_of = []
            for u in range(per_step):
                i = step * per_step + u
                row = {}
                for a in sorted({c // 3 for c in chunk}):
                    for part in (a, 3 + a):
                        wide = jnp.broadcast_to(left[part, pl.ds(i, 1), :], (16, 2 * half)).astype(jnp.bfloat16)
                        row[part] = jnp.concatenate([wide] * (sensors // 16), axis=0)
                terms = [row[c // 3] * right_r[c % 3] + row[3 + c // 3] * right_i[c % 3] for c in chunk]
                blocks_of.append(jnp.concatenate(terms, axis=1))
            products = jnp.concatenate(blocks_of, axis=0)
            columns = pl.ds(pl.multiple_of(step * per_step * sensors, per_step * sensors), per_step * sensors)
            total[:, :width] += jnp.dot(selector[:, columns], products, preferred_element_type=jnp.float32)
            return carried

        total[:, :width] = jnp.zeros((slot_count, width), jnp.float32)
        lax.fori_loop(0, sensors // per_step, add, 0)

    spans = []
    first = 0
    for chunk, _ in CHUNKS:
        spans.append((first, 2 * half * len(chunk)))
        first += 2 * half * len(chunk)
    share = slot_count // groups

    def sums_copy(k, step, source):
        start, width = spans[k]
        to = lax.rem(own_g + step, groups)
        return pltpu.make_async_remote_copy(
            src_ref=send_a.at[pl.ds(pl.multiple_of(to * share, share), share), pl.ds(start, width)],
            dst_ref=recv_a.at[pl.ds(pl.multiple_of(source * share, share), share), pl.ds(start, width)],
            send_sem=a_send.at[k, step], recv_sem=a_recv.at[k, step],
            device_id=(to, own_b), device_id_type=MESH)

    def start_sums(k):
        start, width = spans[k]
        send_a[:, start:start + width] = total[:, :width].astype(jnp.bfloat16)
        for step in range(1, groups):
            sums_copy(k, step, own_g).start()
        own = pl.ds(pl.multiple_of(own_g * share, share), share)
        recv_a[own, start:start + width] = send_a[own, start:start + width]

    def cells_copy(k, step, source):
        start, width = spans[k]
        to = lax.rem(own_b + step, blocks)
        return pltpu.make_async_remote_copy(
            src_ref=send_b.at[to, :, pl.ds(start, width)],
            dst_ref=recv_b.at[source, :, pl.ds(start, width)],
            send_sem=b_send.at[k, step], recv_sem=b_recv.at[k, step],
            device_id=(own_g, to), device_id_type=MESH)

    def start_cells(k):
        start, width = spans[k]
        for step in range(1, groups):
            sums_copy(k, step, lax.rem(own_g - step + groups, groups)).wait_recv()
        count = blocks * cells
        hit = lax.broadcasted_iota(jnp.int32, (count, groups * share), 0) == target_ref[...]
        matches = jnp.where(hit, 1.0, 0.0).astype(jnp.bfloat16)
        stacked = jnp.dot(matches, recv_a[:, start:start + width], preferred_element_type=jnp.float32)
        send_b[:, :, start:start + width] = stacked.astype(jnp.bfloat16).reshape(blocks, cells, width)
        for step in range(1, blocks):
            cells_copy(k, step, own_b).start()
        recv_b[own_b, :, start:start + width] = send_b[own_b, :, start:start + width]

    def transform(k):
        start, width = spans[k]
        for step in range(1, blocks):
            cells_copy(k, step, lax.rem(own_b - step + blocks, blocks)).wait_recv()
        lines = []
        for m in range(len(CHUNKS[k][0])):
            at = start + 2 * half * m
            lines.append(jnp.concatenate([recv_b[b, :, at:at + 2 * half] for b in range(blocks)], axis=1))
        spectrum = jnp.concatenate(lines, axis=0) if len(lines) > 1 else lines[0]
        lag = jnp.dot(spectrum, table[...], preferred_element_type=jnp.float32).astype(jnp.bfloat16)
        for m, c in enumerate(CHUNKS[k][0]):
            out_ref[c] = lag[m * cells:(m + 1) * cells]

    slot_sums(CHUNKS[0][0], CHUNKS[0][1], spans[0][1])
    start_sums(0)
    slot_sums(CHUNKS[1][0], CHUNKS[1][1], spans[1][1])
    start_sums(1)
    start_cells(0)
    slot_sums(CHUNKS[2][0], CHUNKS[2][1], spans[2][1])
    start_sums(2)
    start_cells(1)
    table_copy.wait()
    transform(0)
    start_cells(2)
    transform(1)
    transform(2)

    for step in range(1, blocks):
        bins_copy(step, own_b).wait_send()
    for k in range(len(CHUNKS)):
        for step in range(1, groups):
            sums_copy(k, step, own_g).wait_send()
        for step in range(1, blocks):
            cells_copy(k, step, own_b).wait_send()


def on_device(spectra, pair_slot, slot_cell, cell_rank):
    rows, _, _, freqs = spectra.shape
    groups, slot_count = slot_cell.shape
    blocks = lax.axis_size("partner")
    sensors = rows * blocks
    cells = cell_rank.shape[0] // (groups * blocks)
    own_bins = 2 * freqs // blocks
    width = 9 * own_bins
    share = slot_count // groups

    mine = spectra.reshape(rows, 3, 2, blocks, freqs // blocks).transpose(3, 1, 0, 2, 4)
    mine = mine.reshape(blocks, 3, rows, own_bins)
    ids = jnp.broadcast_to(pair_slot.astype(jnp.bfloat16)[None, None], (blocks, 1, rows, sensors))
    mine = jnp.concatenate([mine, ids], axis=1)

    own_g = lax.axis_index("sensor")
    my_cells = lax.dynamic_slice_in_dim(slot_cell, own_g * share, share, 1)
    ranks = jnp.take(cell_rank, jnp.maximum(my_cells, 0))
    target = jnp.where(my_cells >= 0, ranks - own_g * (blocks * cells), -1).reshape(1, groups * share)

    table = jnp.asarray(lag_table(freqs, blocks))
    count = len(CHUNKS)
    widest = max(len(chunk) for chunk, _ in CHUNKS) * own_bins
    vmem = pl.BlockSpec(memory_space=pltpu.VMEM)
    out = pl.pallas_call(
        functools.partial(kernel, (groups, blocks, rows, cells)),
        out_shape=jax.ShapeDtypeStruct((9, cells, 2 * freqs), jnp.bfloat16),
        in_specs=[vmem, vmem, pl.BlockSpec(memory_space=pl.ANY)],
        out_specs=vmem,
        scratch_shapes=[
            pltpu.VMEM((blocks, 4, rows, own_bins), jnp.bfloat16),
            pltpu.VMEM((6, sensors, own_bins), jnp.float32),
            pltpu.VMEM((3, sensors, own_bins), jnp.bfloat16),
            pltpu.VMEM((3, sensors, own_bins), jnp.bfloat16),
            pltpu.VMEM((sensors, sensors), jnp.float32),
            pltpu.VMEM((slot_count, sensors * sensors), jnp.bfloat16),
            pltpu.VMEM((slot_count, widest), jnp.float32),
            pltpu.VMEM((2 * freqs, 2 * freqs), jnp.bfloat16),
            pltpu.VMEM((slot_count, width), jnp.bfloat16),
            pltpu.VMEM((groups * share, width), jnp.bfloat16),
            pltpu.VMEM((blocks, cells, width), jnp.bfloat16),
            pltpu.VMEM((blocks, cells, width), jnp.bfloat16),
            pltpu.SemaphoreType.DMA,
            pltpu.SemaphoreType.DMA((blocks,)),
            pltpu.SemaphoreType.DMA((blocks,)),
            pltpu.SemaphoreType.DMA((count, groups)),
            pltpu.SemaphoreType.DMA((count, groups)),
            pltpu.SemaphoreType.DMA((count, blocks)),
            pltpu.SemaphoreType.DMA((count, blocks)),
        ],
        compiler_params=pltpu.CompilerParams(
            collective_id=0, has_side_effects=True, vmem_limit_bytes=56 * 2**20),
        name="stack_pairs",
    )(mine, target, table)
    return out.transpose(1, 0, 2)


def solution(mesh):
    in_specs = (
        P(("sensor", "partner"), None, None, None),
        P(("sensor", "partner"), None),
        P(),
        P(),
    )
    out_specs = P(("sensor", "partner"), None, None)
    return jax.shard_map(
        on_device, mesh=mesh, in_specs=in_specs, out_specs=out_specs, check_vma=False
    )
```

time: 261 us -> 49.7 us (0.19)
  other arithmetic: 80.8 us -> 2.24 us
  local copies, waits for them, and re-layouts: 62.2 us -> 4.96 us
  waiting for transfers between devices: 48 us -> 0 us
  matrix products: 43.1 us -> 0 us
  Pallas kernels: 0 us -> 42.2 us
  blocking collectives: 15.2 us -> 0 us
  starting transfers between devices: 9.94 us -> 0 us
    another operation x4 -> x0, other arithmetic: 57.2 us -> none  [the longest x2 33.1 us: cross_spectra(): joined = jnp.stack([real_part, imag_part], axis=4)]
    another operation x2 -> x0, local copies, waits for them, and re-layouts: 52.2 us -> none  [cross_spectra(): joined = jnp.stack([real_part, imag_part], axis=4)]
    all_to_all x1 -> x0, waiting for transfers between devices: 48 us -> none  [on_device(): lax.all_to_all(partial_value.astype(jnp.bfloat16), ('sensor', 'partner'),...]
    dot_general x4 -> x0, matrix products: 43.1 us -> none  [the longest x2 35.2 us: add_block(): jnp.einsum('ps,px->sx', selector, products, preferred_element_type=jnp.fl...]
    pallas_call x0 -> x1, Pallas kernels: none -> 42.2 us  [on_device(): pl.pallas_call(functools.partial(kernel, (groups, blocks, rows, cells)),...]
    all_gather x1 -> x0, blocking collectives: 15.2 us -> none  [on_device(): piece = lax.all_gather(spectra, 'partner', axis=0, tiled=True)]
    all_to_all x1 -> x0, starting transfers between devices: 9.94 us -> none  [on_device(): lax.all_to_all(partial_value.astype(jnp.bfloat16), ('sensor', 'partner'),...]
    cos x1 -> x0, other arithmetic: 9.32 us -> none  [lag_table(): return jnp.concatenate([jnp.cos(angle), -jnp.sin(angle)], axis=0) / freqs]
  transfers between devices with their start and end apart: 1 -> 0, of which waited for: 1 -> 0; matrix products, arithmetic and copies ran while one was open for 4% -> 0% of each run, Pallas kernels for 0% -> 0%
where the time goes in v1:
time: 49.7 us; the launch traced here: 49.4 us
  Pallas kernels  42.2 us (85%)
  local copies, waits for them, and re-layouts  4.96 us (10%)
  other arithmetic  2.24 us (5%)
    pallas_call x1, Pallas kernels, on_device(): pl.pallas_call(functools.partial(kernel, (groups, blocks, rows, cells)),...  42.2 us
    unnamed x7, local copies, waits for them, and re-layouts  1.93 us
    gather x2, local copies, waits for them, and re-layouts, on_device(): ranks = jnp.take(cell_rank, jnp.maximum(my_cells, 0))  1.8 us

profile of v1, /device:TPU:1, one launch (start us, length us, event | category | flops | bytes accessed | tf_op | source)
XLA Modules:
  0.0 49.4 jit_solution(5256169172202060827)
XLA Ops:
  0.0 0.0 copy-start
  0.0 0.7 %convert_element_type.3 = bf16[16,128]{1,0:T(8,128)(2,1)S(1)} convert(s32[16,128]{1,0:T(8,128)} %param.6) | non-fusion elementwise | flops 2048 | bytes 12288 | tf_op jit(solution)/shard_map/convert_element_type | solution.py:192
  0.7 0.8 %dynamic-slice_maximum_fusion = s32[16,16]{1,0:T(8,128)S(1)} fusion(s32[16,256]{1,0:T(8,128)} %param.7, s32[]{:T(128)S(6)} %select_n.14), kind=kLoop, calls=%fused_computation.4 | loop fusion | flops 256 | bytes 2052 | tf_op jit(solution)/shard_map/max | solution.py:197
  1.5 0.1 reshape.22
  1.6 0.0 copy-done
  1.6 0.0 copy-start.2
  1.6 0.0 copy-start.1
  1.6 1.7 %gather_fusion = s32[256]{0:T(256)S(1)} fusion(s32[4096]{0:T(1024)S(1)} %copy-done, s32[1024]{0:T(1024)S(1)} %pad_clamp_fusion), kind=kCustom, calls=%fused_computation | custom fusion | bytes 3072 | tf_op jit(solution)/shard_map/jit(_take)/gather | solution.py:197
  3.3 0.1 reshape.21
  3.4 0.0 copy-done.2
  3.4 0.1 subtract_select_fusion
  3.5 0.7 %reshape.19.target_ref = s32[1,256]{1,0:T(1,128)} reshape(s32[16,16]{1,0:T(8,128)S(1)} %subtract_select_fusion) | data formatting | bytes 2048 | tf_op jit(solution)/shard_map/reshape | solution.py:198
  4.2 0.0 copy-done.1
  4.2 0.2 reshape.17
  4.4 0.2 copy.9
  4.5 0.1 reshape.18
  4.7 0.7 %pad_maximum_fusion.mine_ref = bf16[8,4,16,128]{3,2,1,0:T(8,128)(2,1)} fusion(bf16[8,1,16,128]{3,2,1,0:T(8,128)(2,1)S(1)} %broadcast_in_dim.18, bf16[8,3,16,128]{3,2,1,0:T(8,128)(2,1)S(1)} %reshape.18), kind=kLoop, calls=%fused_computation.2 | loop fusion | flops 65536 | bytes 262144 | tf_op jit(solution)/shard_map/concatenate | solution.py:193
  5.3 42.2 %stack_pairs.1 = bf16[9,32,1024]{2,1,0:T(8,128)(2,1)} custom-call(bf16[8,4,16,128]{3,2,1,0:T(8,128)(2,1)} %pad_maximum_fusion.mine_ref, s32[1,256]{1,0:T(1,128)} %reshape.19.target_ref, bf16[1024,1024]{1,0:T(8,128)(2,1)} %constant.33.clone.table_hbm), custom_call_target="tpu_custom_call" | custom-call | tf_op jit(solution)/shard_map/stack_pairs/pallas_call | solution.py:204
  47.5 1.9 %copy.11 = bf16[32,9,1024]{2,0,1:T(8,128)(2,1)} copy(bf16[32,9,1024]{2,0,1:T(8,128)(2,1)} %bitcast.4) | data formatting | bytes 1179648
  (2 shorter events, 0.0 us)
Async XLA Ops:
  0.0 1.6 %copy-start = (s32[4096]{0:T(1024)S(1)}, s32[4096]{0:T(1024)}, u32[]{:S(2)}) copy-start(s32[4096]{0:T(1024)} %param.8) | copy-start | bytes 49156
  1.6 1.8 %copy-start.2 = (s32[16,256]{1,0:T(8,128)S(1)}, s32[16,256]{1,0:T(8,128)}, u32[]{:S(2)}) copy-start(s32[16,256]{1,0:T(8,128)} %param.7) | copy-start | bytes 49156
  1.6 2.6 %copy-start.1 = (bf16[16,3,2,512]{3,2,1,0:T(2,128)(2,1)S(1)}, bf16[16,3,2,512]{3,2,1,0:T(2,128)(2,1)}, u32[]{:S(2)}) copy-start(bf16[16,3,2,512]{3,2,1,0:T(2,128)(2,1)} %param.5) | copy-start | bytes 294916

commit v2 on v1

--- a/solution.py
+++ b/solution.py
@@ -10,7 +10,7 @@
 from jax.sharding import PartitionSpec as P
 
 MESH = pl.DeviceIdType.MESH
-CHUNKS = (((0, 1, 2, 3), 32), ((4, 5, 6, 7), 32), ((8,), 64))
+CHUNKS = (((8,), 64), ((0, 1), 64), ((2, 3), 64), ((4, 5), 64), ((6, 7), 64))
 
 
 def lag_table(freqs, blocks):
@@ -23,33 +23,79 @@
     return both.reshape(2 * freqs, lags).astype(jnp.bfloat16)
 
 
-def kernel(sizes, mine_ref, target_ref, table_hbm, out_ref, got, left, right_r, right_i, slots,
-           selector, total, table, send_a, recv_a, send_b, recv_b, table_sem,
+def one_hot(condition):
+    return jnp.where(condition, 1.0, 0.0).astype(jnp.bfloat16)
+
+
+def cell_rows(slot_cell, rank_table, own_g, share, blocks, cells):
+    groups, slot_count = slot_cell.shape
+    span = rank_table.shape[1]
+    count = groups * share
+    of_slot = lax.broadcasted_iota(jnp.int32, (slot_count, count), 0)
+    incoming = lax.broadcasted_iota(jnp.int32, (slot_count, count), 1)
+    pick = one_hot(of_slot == own_g * share + incoming % share)
+    used = slot_cell >= 0
+    high = jnp.where(used, slot_cell // span, -1).astype(jnp.float32).astype(jnp.bfloat16)
+    low = jnp.where(used, slot_cell % span, 0).astype(jnp.float32).astype(jnp.bfloat16)
+    group = lax.broadcasted_iota(jnp.int32, (groups, count), 0)
+    mine = group == lax.broadcasted_iota(jnp.int32, (groups, count), 1) // share
+
+    def own(values):
+        spread = jnp.dot(values, pick, preferred_element_type=jnp.float32)
+        return jnp.sum(jnp.where(mine, spread, 0.0), axis=0, keepdims=True)
+
+    high, low = own(high), own(low)
+    place = (rank_table % cells).astype(jnp.float32).astype(jnp.bfloat16)
+    low_ids = lax.broadcasted_iota(jnp.int32, (span, count), 0).astype(jnp.float32)
+    spread = jnp.dot(place, one_hot(low_ids == low), preferred_element_type=jnp.float32)
+    high_ids = lax.broadcasted_iota(jnp.int32, (rank_table.shape[0], count), 0).astype(jnp.float32)
+    place = jnp.sum(jnp.where(high_ids == high, spread, 0.0), axis=0, keepdims=True)
+    owner = lax.broadcasted_iota(jnp.int32, (1, count), 1) % share // (share // blocks)
+    return jnp.where(high >= 0, place + (owner * cells).astype(jnp.float32), -1.0)
+
+
+def kernel(sizes, spectra_ref, pair_slot_ref, slot_cell_ref, rank_ref, table_hbm, out_ref, mine, got, left, right_r,
+           right_i, slots, selector, total, matches, table, send_a, recv_a, send_b, recv_b, table_sem,
            x_send, x_recv, a_send, a_recv, b_send, b_recv):
     groups, blocks, rows, cells = sizes
     sensors = blocks * rows
     own_g, own_b = lax.axis_index("sensor"), lax.axis_index("partner")
     half = out_ref.shape[2] // blocks // 2
 
+    barrier = pltpu.get_barrier_semaphore()
+    for step in range(1, groups):
+        pl.semaphore_signal(barrier, inc=1, device_id=(lax.rem(own_g + step, groups), own_b), device_id_type=MESH)
+    for step in range(1, blocks):
+        pl.semaphore_signal(barrier, inc=1, device_id=(own_g, lax.rem(own_b + step, blocks)), device_id_type=MESH)
     table_copy = pltpu.make_async_copy(table_hbm, table, table_sem)
     table_copy.start()
 
-    barrier = pltpu.get_barrier_semaphore()
-    for step in range(1, blocks):
-        pl.semaphore_signal(barrier, inc=1, device_id=(own_g, lax.rem(own_b + step, blocks)), device_id_type=MESH)
-    for step in range(1, groups):
-        pl.semaphore_signal(barrier, inc=1, device_id=(lax.rem(own_g + step, groups), own_b), device_id_type=MESH)
+    ids = pair_slot_ref[...].astype(jnp.float32).astype(jnp.bfloat16)
+    first = lax.broadcasted_iota(jnp.int32, (rows, 2 * half), 1) < half
+    for a in range(3):
+        for pair in range(blocks // 2):
+            lanes = slice(pair * 2 * half, (pair + 1) * 2 * half)
+            real = spectra_ref[:, a, 0, lanes].astype(jnp.float32)
+            imag = spectra_ref[:, a, 1, lanes].astype(jnp.float32)
+            mine[2 * pair, a] = jnp.where(first, real, pltpu.roll(imag, half, 1)).astype(jnp.bfloat16)
+            mine[2 * pair + 1, a] = jnp.where(first, pltpu.roll(real, half, 1), imag).astype(jnp.bfloat16)
+    for b in range(blocks):
+        mine[b, 3] = ids
+    share = slot_cell_ref.shape[1] // groups
+    at = cell_rows(slot_cell_ref[...], rank_ref[...], own_g, share, blocks, cells)
+    row_ids = lax.broadcasted_iota(jnp.int32, (blocks * cells, groups * share), 0).astype(jnp.float32)
+    matches[...] = one_hot(row_ids == at)
     pl.semaphore_wait(barrier, blocks + groups - 2)
 
     def bins_copy(step, source):
         to = lax.rem(own_b + step, blocks)
         return pltpu.make_async_remote_copy(
-            src_ref=mine_ref.at[to], dst_ref=got.at[source], send_sem=x_send.at[step], recv_sem=x_recv.at[step],
+            src_ref=mine.at[to], dst_ref=got.at[source], send_sem=x_send.at[step], recv_sem=x_recv.at[step],
             device_id=(own_g, to), device_id_type=MESH)
 
     for step in range(1, blocks):
         bins_copy(step, own_b).start()
-    got[own_b] = mine_ref[own_b]
+    got[own_b] = mine[own_b]
     for step in range(1, blocks):
         bins_copy(step, lax.rem(own_b - step + blocks, blocks)).wait_recv()
 
@@ -64,18 +110,17 @@
     slots[...] = got[:, 3].reshape(sensors, sensors).astype(jnp.float32)
 
     slot_count = selector.shape[0]
-    ids = lax.broadcasted_iota(jnp.int32, (slot_count, sensors), 0).astype(jnp.float32).astype(jnp.bfloat16)
-
-    def select(i, carried):
+    slot_ids = lax.broadcasted_iota(jnp.int32, (slot_count, sensors), 0).astype(jnp.float32).astype(jnp.bfloat16)
+
+    def select(i):
         row = jnp.broadcast_to(slots[pl.ds(i, 1), :], (16, sensors)).astype(jnp.bfloat16)
         row = jnp.concatenate([row] * (slot_count // 16), axis=0)
-        columns = pl.ds(pl.multiple_of(i * sensors, sensors), sensors)
-        selector[:, columns] = jnp.where(row == ids, jnp.bfloat16(1), jnp.bfloat16(0))
-        return carried
-
-    lax.fori_loop(0, sensors, select, 0)
-
-    def slot_sums(chunk, per_step, width):
+        return jnp.where(row == slot_ids, jnp.bfloat16(1), jnp.bfloat16(0))
+
+    def slot_sums(k):
+        chunk, per_step = CHUNKS[k]
+        width = spans[k][1]
+
         def add(step, carried):
             blocks_of = []
             for u in range(per_step):
@@ -89,7 +134,12 @@
                 blocks_of.append(jnp.concatenate(terms, axis=1))
             products = jnp.concatenate(blocks_of, axis=0)
             columns = pl.ds(pl.multiple_of(step * per_step * sensors, per_step * sensors), per_step * sensors)
-            total[:, :width] += jnp.dot(selector[:, columns], products, preferred_element_type=jnp.float32)
+            if k == 0:
+                chosen = jnp.concatenate([select(step * per_step + u) for u in range(per_step)], axis=1)
+                selector[:, columns] = chosen
+            else:
+                chosen = selector[:, columns]
+            total[:, :width] += jnp.dot(chosen, products, preferred_element_type=jnp.float32)
             return carried
 
         total[:, :width] = jnp.zeros((slot_count, width), jnp.float32)
@@ -100,7 +150,6 @@
     for chunk, _ in CHUNKS:
         spans.append((first, 2 * half * len(chunk)))
         first += 2 * half * len(chunk)
-    share = slot_count // groups
 
     def sums_copy(k, step, source):
         start, width = spans[k]
@@ -132,10 +181,7 @@
         start, width = spans[k]
         for step in range(1, groups):
             sums_copy(k, step, lax.rem(own_g - step + groups, groups)).wait_recv()
-        count = blocks * cells
-        hit = lax.broadcasted_iota(jnp.int32, (count, groups * share), 0) == target_ref[...]
-        matches = jnp.where(hit, 1.0, 0.0).astype(jnp.bfloat16)
-        stacked = jnp.dot(matches, recv_a[:, start:start + width], preferred_element_type=jnp.float32)
+        stacked = jnp.dot(matches[...], recv_a[:, start:start + width], preferred_element_type=jnp.float32)
         send_b[:, :, start:start + width] = stacked.astype(jnp.bfloat16).reshape(blocks, cells, width)
         for step in range(1, blocks):
             cells_copy(k, step, own_b).start()
@@ -154,23 +200,21 @@
         for m, c in enumerate(CHUNKS[k][0]):
             out_ref[c] = lag[m * cells:(m + 1) * cells]
 
-    slot_sums(CHUNKS[0][0], CHUNKS[0][1], spans[0][1])
-    start_sums(0)
-    slot_sums(CHUNKS[1][0], CHUNKS[1][1], spans[1][1])
-    start_sums(1)
-    start_cells(0)
-    slot_sums(CHUNKS[2][0], CHUNKS[2][1], spans[2][1])
-    start_sums(2)
-    start_cells(1)
+    count = len(CHUNKS)
+    for k in range(count):
+        slot_sums(k)
+        start_sums(k)
+        if k >= 1:
+            start_cells(k - 1)
     table_copy.wait()
-    transform(0)
-    start_cells(2)
-    transform(1)
-    transform(2)
+    for k in range(count - 1):
+        transform(k)
+    start_cells(count - 1)
+    transform(count - 1)
 
     for step in range(1, blocks):
         bins_copy(step, own_b).wait_send()
-    for k in range(len(CHUNKS)):
+    for k in range(count):
         for step in range(1, groups):
             sums_copy(k, step, own_g).wait_send()
         for step in range(1, blocks):
@@ -187,16 +231,6 @@
     width = 9 * own_bins
     share = slot_count // groups
 
-    mine = spectra.reshape(rows, 3, 2, blocks, freqs // blocks).transpose(3, 1, 0, 2, 4)
-    mine = mine.reshape(blocks, 3, rows, own_bins)
-    ids = jnp.broadcast_to(pair_slot.astype(jnp.bfloat16)[None, None], (blocks, 1, rows, sensors))
-    mine = jnp.concatenate([mine, ids], axis=1)
-
-    own_g = lax.axis_index("sensor")
-    my_cells = lax.dynamic_slice_in_dim(slot_cell, own_g * share, share, 1)
-    ranks = jnp.take(cell_rank, jnp.maximum(my_cells, 0))
-    target = jnp.where(my_cells >= 0, ranks - own_g * (blocks * cells), -1).reshape(1, groups * share)
-
     table = jnp.asarray(lag_table(freqs, blocks))
     count = len(CHUNKS)
     widest = max(len(chunk) for chunk, _ in CHUNKS) * own_bins
@@ -204,9 +238,10 @@
     out = pl.pallas_call(
         functools.partial(kernel, (groups, blocks, rows, cells)),
         out_shape=jax.ShapeDtypeStruct((9, cells, 2 * freqs), jnp.bfloat16),
-        in_specs=[vmem, vmem, pl.BlockSpec(memory_space=pl.ANY)],
+        in_specs=[vmem, vmem, vmem, vmem, pl.BlockSpec(memory_space=pl.ANY)],
         out_specs=vmem,
         scratch_shapes=[
+            pltpu.VMEM((blocks, 4, rows, own_bins), jnp.bfloat16),
             pltpu.VMEM((blocks, 4, rows, own_bins), jnp.bfloat16),
             pltpu.VMEM((6, sensors, own_bins), jnp.float32),
             pltpu.VMEM((3, sensors, own_bins), jnp.bfloat16),
@@ -214,6 +249,7 @@
             pltpu.VMEM((sensors, sensors), jnp.float32),
             pltpu.VMEM((slot_count, sensors * sensors), jnp.bfloat16),
             pltpu.VMEM((slot_count, widest), jnp.float32),
+            pltpu.VMEM((blocks * cells, groups * share), jnp.bfloat16),
             pltpu.VMEM((2 * freqs, 2 * freqs), jnp.bfloat16),
             pltpu.VMEM((slot_count, width), jnp.bfloat16),
             pltpu.VMEM((groups * share, width), jnp.bfloat16),
@@ -230,7 +266,7 @@
         compiler_params=pltpu.CompilerParams(
             collective_id=0, has_side_effects=True, vmem_limit_bytes=56 * 2**20),
         name="stack_pairs",
-    )(mine, target, table)
+    )(spectra, pair_slot, slot_cell, cell_rank.reshape(-1, 128), table)
     return out.transpose(1, 0, 2)
 
 

time: 49.7 us -> 46.9 us (0.944)
  local copies, waits for them, and re-layouts: 4.96 us -> 1.92 us
  Pallas kernels: 42.2 us -> 44.8 us
  other arithmetic: 2.24 us -> 0 us
    pallas_call x1, Pallas kernels: 42.2 us -> 44.8 us  [on_device(): pl.pallas_call(functools.partial(kernel, (groups, blocks, rows, cells)),...]
    gather x2 -> x0, local copies, waits for them, and re-layouts: 1.8 us -> none  [on_device(): ranks = jnp.take(cell_rank, jnp.maximum(my_cells, 0))]
    reshape x4 -> x0, local copies, waits for them, and re-layouts: 1.14 us -> none  [the longest x1 0.68 us: on_device(): jnp.where(my_cells >= 0, ranks - own_g * (blocks * cells), -1)]
    max x1 -> x0, other arithmetic: 0.77 us -> none  [on_device(): ranks = jnp.take(cell_rank, jnp.maximum(my_cells, 0))]
    convert_element_type x1 -> x0, other arithmetic: 0.71 us -> none  [on_device(): pair_slot.astype(jnp.bfloat16)[None, None]]
    concatenate x1 -> x0, other arithmetic: 0.67 us -> none  [on_device(): mine = jnp.concatenate([mine, ids], axis=1)]
    unnamed x7 -> x1, local copies, waits for them, and re-layouts: 1.93 us -> 1.92 us
where the time goes in v2:
time: 46.9 us; the launch traced here: 46.8 us
  Pallas kernels  44.8 us (96%)
  local copies, waits for them, and re-layouts  1.92 us (4%)
    pallas_call x1, Pallas kernels, on_device(): pl.pallas_call(functools.partial(kernel, (groups, blocks, rows, cells)),...  44.8 us
    unnamed x1, local copies, waits for them, and re-layouts  1.92 us

profile of v2, /device:TPU:1, one launch (start us, length us, event | category | flops | bytes accessed | tf_op | source)
XLA Modules:
  0.0 46.8 jit_solution(5078272057311714768)
XLA Ops:
  0.0 44.8 %stack_pairs.1 = bf16[9,32,1024]{2,1,0:T(8,128)(2,1)} custom-call(bf16[16,3,2,512]{3,2,1,0:T(2,128)(2,1)} %spectra_ref.1, s32[16,128]{1,0:T(8,128)} %pair_slot_ref.1, s32[16,256]{1,0:T(8,128)} %slot_cell_ref.1, s32[32,128]{1,0:T(8,128)} %bitcast.3, bf16[1024,1024]{1,0:T(8,128)(2,1)} %constant.2.clone.table_hbm), custom_call_target="tpu_custom_call" | custom-call | tf_op jit(solution)/shard_map/stack_pairs/pallas_call | solution.py:238
  44.9 1.9 %copy.7 = bf16[32,9,1024]{2,0,1:T(8,128)(2,1)} copy(bf16[32,9,1024]{2,0,1:T(8,128)(2,1)} %bitcast.2) | data formatting | bytes 1179648

commit v3 on v2

--- a/solution.py
+++ b/solution.py
@@ -10,7 +10,7 @@
 from jax.sharding import PartitionSpec as P
 
 MESH = pl.DeviceIdType.MESH
-CHUNKS = (((8,), 64), ((0, 1), 64), ((2, 3), 64), ((4, 5), 64), ((6, 7), 64))
+CHUNKS = (((0, 1, 2, 3,4,5), 32), ((6, 7,8), 32))
 
 
 def lag_table(freqs, blocks):
@@ -54,12 +54,24 @@
     return jnp.where(high >= 0, place + (owner * cells).astype(jnp.float32), -1.0)
 
 
-def kernel(sizes, spectra_ref, pair_slot_ref, slot_cell_ref, rank_ref, table_hbm, out_ref, mine, got, left, right_r,
-           right_i, slots, selector, total, matches, table, send_a, recv_a, send_b, recv_b, table_sem,
+def wait_for(ref, semaphore):
+    pltpu.make_async_copy(ref, ref, semaphore).wait()
+
+
+def kernel(sizes, spectra_hbm, pair_slot_hbm, slot_cell_hbm, rank_hbm, table_hbm, out_ref, spectra_ref, pair_slot_ref,
+           slot_cell_ref, rank_ref, in_sems, mine, got, left, right_r,
+           right_i, slots, total, matches, table, send_a, recv_a, send_b, recv_b, table_sem,
            x_send, x_recv, a_send, a_recv, b_send, b_recv):
     groups, blocks, rows, cells = sizes
     sensors = blocks * rows
     own_g, own_b = lax.axis_index("sensor"), lax.axis_index("partner")
+    inputs = [
+        pltpu.make_async_copy(source, to, in_sems.at[n])
+        for n, (source, to) in enumerate((
+            (spectra_hbm, spectra_ref), (pair_slot_hbm, pair_slot_ref), (slot_cell_hbm, slot_cell_ref), (rank_hbm, rank_ref)))
+    ]
+    for copy in inputs:
+        copy.start()
     half = out_ref.shape[2] // blocks // 2
 
     barrier = pltpu.get_barrier_semaphore()
@@ -70,6 +82,8 @@
     table_copy = pltpu.make_async_copy(table_hbm, table, table_sem)
     table_copy.start()
 
+    for copy in inputs:
+        copy.wait()
     ids = pair_slot_ref[...].astype(jnp.float32).astype(jnp.bfloat16)
     first = lax.broadcasted_iota(jnp.int32, (rows, 2 * half), 1) < half
     for a in range(3):
@@ -87,17 +101,17 @@
     matches[...] = one_hot(row_ids == at)
     pl.semaphore_wait(barrier, blocks + groups - 2)
 
-    def bins_copy(step, source):
+    def bins_copy(step):
         to = lax.rem(own_b + step, blocks)
         return pltpu.make_async_remote_copy(
-            src_ref=mine.at[to], dst_ref=got.at[source], send_sem=x_send.at[step], recv_sem=x_recv.at[step],
+            src_ref=mine.at[to], dst_ref=got.at[own_b], send_sem=x_send, recv_sem=x_recv,
             device_id=(own_g, to), device_id_type=MESH)
 
     for step in range(1, blocks):
-        bins_copy(step, own_b).start()
+        bins_copy(step).start()
     got[own_b] = mine[own_b]
-    for step in range(1, blocks):
-        bins_copy(step, lax.rem(own_b - step + blocks, blocks)).wait_recv()
+    others = got.at[pl.ds(0, blocks - 1)]
+    wait_for(others, x_recv)
 
     low = lax.broadcasted_iota(jnp.int32, (sensors, 2 * half), 1) < half
     for a in range(3):
@@ -109,7 +123,7 @@
         right_i[a] = jnp.where(low, swapped, x).astype(jnp.bfloat16)
     slots[...] = got[:, 3].reshape(sensors, sensors).astype(jnp.float32)
 
-    slot_count = selector.shape[0]
+    slot_count = total.shape[0]
     slot_ids = lax.broadcasted_iota(jnp.int32, (slot_count, sensors), 0).astype(jnp.float32).astype(jnp.bfloat16)
 
     def select(i):
@@ -133,12 +147,7 @@
                 terms = [row[c // 3] * right_r[c % 3] + row[3 + c // 3] * right_i[c % 3] for c in chunk]
                 blocks_of.append(jnp.concatenate(terms, axis=1))
             products = jnp.concatenate(blocks_of, axis=0)
-            columns = pl.ds(pl.multiple_of(step * per_step * sensors, per_step * sensors), per_step * sensors)
-            if k == 0:
-                chosen = jnp.concatenate([select(step * per_step + u) for u in range(per_step)], axis=1)
-                selector[:, columns] = chosen
-            else:
-                chosen = selector[:, columns]
+            chosen = jnp.concatenate([select(step * per_step + u) for u in range(per_step)], axis=1)
             total[:, :width] += jnp.dot(chosen, products, preferred_element_type=jnp.float32)
             return carried
 
@@ -151,46 +160,44 @@
         spans.append((first, 2 * half * len(chunk)))
         first += 2 * half * len(chunk)
 
-    def sums_copy(k, step, source):
+    def sums_copy(k, step):
         start, width = spans[k]
         to = lax.rem(own_g + step, groups)
         return pltpu.make_async_remote_copy(
             src_ref=send_a.at[pl.ds(pl.multiple_of(to * share, share), share), pl.ds(start, width)],
-            dst_ref=recv_a.at[pl.ds(pl.multiple_of(source * share, share), share), pl.ds(start, width)],
-            send_sem=a_send.at[k, step], recv_sem=a_recv.at[k, step],
+            dst_ref=recv_a.at[pl.ds(pl.multiple_of(own_g * share, share), share), pl.ds(start, width)],
+            send_sem=a_send.at[k], recv_sem=a_recv.at[k],
             device_id=(to, own_b), device_id_type=MESH)
 
     def start_sums(k):
         start, width = spans[k]
         send_a[:, start:start + width] = total[:, :width].astype(jnp.bfloat16)
         for step in range(1, groups):
-            sums_copy(k, step, own_g).start()
+            sums_copy(k, step).start()
         own = pl.ds(pl.multiple_of(own_g * share, share), share)
         recv_a[own, start:start + width] = send_a[own, start:start + width]
 
-    def cells_copy(k, step, source):
+    def cells_copy(k, step):
         start, width = spans[k]
         to = lax.rem(own_b + step, blocks)
         return pltpu.make_async_remote_copy(
             src_ref=send_b.at[to, :, pl.ds(start, width)],
-            dst_ref=recv_b.at[source, :, pl.ds(start, width)],
-            send_sem=b_send.at[k, step], recv_sem=b_recv.at[k, step],
+            dst_ref=recv_b.at[own_b, :, pl.ds(start, width)],
+            send_sem=b_send.at[k], recv_sem=b_recv.at[k],
             device_id=(own_g, to), device_id_type=MESH)
 
     def start_cells(k):
         start, width = spans[k]
-        for step in range(1, groups):
-            sums_copy(k, step, lax.rem(own_g - step + groups, groups)).wait_recv()
+        wait_for(recv_a.at[pl.ds(0, (groups - 1) * share), pl.ds(start, width)], a_recv.at[k])
         stacked = jnp.dot(matches[...], recv_a[:, start:start + width], preferred_element_type=jnp.float32)
         send_b[:, :, start:start + width] = stacked.astype(jnp.bfloat16).reshape(blocks, cells, width)
         for step in range(1, blocks):
-            cells_copy(k, step, own_b).start()
+            cells_copy(k, step).start()
         recv_b[own_b, :, start:start + width] = send_b[own_b, :, start:start + width]
 
     def transform(k):
         start, width = spans[k]
-        for step in range(1, blocks):
-            cells_copy(k, step, lax.rem(own_b - step + blocks, blocks)).wait_recv()
+        wait_for(recv_b.at[pl.ds(0, blocks - 1), :, pl.ds(start, width)], b_recv.at[k])
         lines = []
         for m in range(len(CHUNKS[k][0])):
             at = start + 2 * half * m
@@ -207,18 +214,19 @@
         if k >= 1:
             start_cells(k - 1)
     table_copy.wait()
-    for k in range(count - 1):
+    for k in range(count - 2):
         transform(k)
+    wait_for(others, x_send)
     start_cells(count - 1)
+    transform(count - 2)
+    for k in range(count):
+        start, width = spans[k]
+        wait_for(send_a.at[pl.ds(0, (groups - 1) * share), pl.ds(start, width)], a_send.at[k])
+        if k < count - 1:
+            wait_for(send_b.at[pl.ds(0, blocks - 1), :, pl.ds(start, width)], b_send.at[k])
     transform(count - 1)
-
-    for step in range(1, blocks):
-        bins_copy(step, own_b).wait_send()
-    for k in range(count):
-        for step in range(1, groups):
-            sums_copy(k, step, own_g).wait_send()
-        for step in range(1, blocks):
-            cells_copy(k, step, own_b).wait_send()
+    start, width = spans[count - 1]
+    wait_for(send_b.at[pl.ds(0, blocks - 1), :, pl.ds(start, width)], b_send.at[count - 1])
 
 
 def on_device(spectra, pair_slot, slot_cell, cell_rank):
@@ -237,17 +245,21 @@
     vmem = pl.BlockSpec(memory_space=pltpu.VMEM)
     out = pl.pallas_call(
         functools.partial(kernel, (groups, blocks, rows, cells)),
-        out_shape=jax.ShapeDtypeStruct((9, cells, 2 * freqs), jnp.bfloat16),
-        in_specs=[vmem, vmem, vmem, vmem, pl.BlockSpec(memory_space=pl.ANY)],
+        out_shape=pltpu.VMEM((9, cells, 2 * freqs), jnp.bfloat16),
+        in_specs=[pl.BlockSpec(memory_space=pl.ANY)] * 5,
         out_specs=vmem,
         scratch_shapes=[
+            pltpu.VMEM(spectra.shape, spectra.dtype),
+            pltpu.VMEM(pair_slot.shape, pair_slot.dtype),
+            pltpu.VMEM(slot_cell.shape, slot_cell.dtype),
+            pltpu.VMEM((cell_rank.shape[0] // 128, 128), cell_rank.dtype),
+            pltpu.SemaphoreType.DMA((4,)),
             pltpu.VMEM((blocks, 4, rows, own_bins), jnp.bfloat16),
             pltpu.VMEM((blocks, 4, rows, own_bins), jnp.bfloat16),
             pltpu.VMEM((6, sensors, own_bins), jnp.float32),
             pltpu.VMEM((3, sensors, own_bins), jnp.bfloat16),
             pltpu.VMEM((3, sensors, own_bins), jnp.bfloat16),
             pltpu.VMEM((sensors, sensors), jnp.float32),
-            pltpu.VMEM((slot_count, sensors * sensors), jnp.bfloat16),
             pltpu.VMEM((slot_count, widest), jnp.float32),
             pltpu.VMEM((blocks * cells, groups * share), jnp.bfloat16),
             pltpu.VMEM((2 * freqs, 2 * freqs), jnp.bfloat16),
@@ -256,12 +268,12 @@
             pltpu.VMEM((blocks, cells, width), jnp.bfloat16),
             pltpu.VMEM((blocks, cells, width), jnp.bfloat16),
             pltpu.SemaphoreType.DMA,
-            pltpu.SemaphoreType.DMA((blocks,)),
-            pltpu.SemaphoreType.DMA((blocks,)),
-            pltpu.SemaphoreType.DMA((count, groups)),
-            pltpu.SemaphoreType.DMA((count, groups)),
-            pltpu.SemaphoreType.DMA((count, blocks)),
-            pltpu.SemaphoreType.DMA((count, blocks)),
+            pltpu.SemaphoreType.DMA,
+            pltpu.SemaphoreType.DMA,
+            pltpu.SemaphoreType.DMA((count,)),
+            pltpu.SemaphoreType.DMA((count,)),
+            pltpu.SemaphoreType.DMA((count,)),
+            pltpu.SemaphoreType.DMA((count,)),
         ],
         compiler_params=pltpu.CompilerParams(
             collective_id=0, has_side_effects=True, vmem_limit_bytes=56 * 2**20),

time: 46.9 us -> 37 us (0.79)
  Pallas kernels: 44.8 us -> 36.1 us
  local copies, waits for them, and re-layouts: 1.92 us -> 0.82 us
    pallas_call x1, Pallas kernels: 44.8 us -> 36.1 us  [on_device(): pl.pallas_call(functools.partial(kernel, (groups, blocks, rows, cells)),...]
    unnamed x1, local copies, waits for them, and re-layouts: 1.92 us -> 0.82 us
where the time goes in v3:
time: 37 us; the launch traced here: 36.9 us
  Pallas kernels  36.1 us (98%)
  local copies, waits for them, and re-layouts  0.82 us (2%)
    pallas_call x1, Pallas kernels, on_device(): pl.pallas_call(functools.partial(kernel, (groups, blocks, rows, cells)),...  36.1 us
    unnamed x1, local copies, waits for them, and re-layouts  0.82 us

profile of v3, /device:TPU:1, one launch (start us, length us, event | category | flops | bytes accessed | tf_op | source)
XLA Modules:
  0.0 36.9 jit_solution(8949564786663884304)
XLA Ops:
  0.0 36.1 %stack_pairs.1 = bf16[9,32,1024]{2,1,0:T(8,128)(2,1)S(1)} custom-call(bf16[16,3,2,512]{3,2,1,0:T(2,128)(2,1)} %spectra_hbm.1, s32[16,128]{1,0:T(8,128)} %pair_slot_hbm.1, s32[16,256]{1,0:T(8,128)} %slot_cell_hbm.1, s32[32,128]{1,0:T(8,128)} %bitcast.3, bf16[1024,1024]{1,0:T(8,128)(2,1)} %constant.2.clone.table_hbm), custom_call_target="tpu_custom_call" | custom-call | tf_op jit(solution)/shard_map/stack_pairs/pallas_call | solution.py:246
  36.1 0.8 %copy.7 = bf16[32,9,1024]{2,0,1:T(8,128)(2,1)} copy(bf16[32,9,1024]{2,0,1:T(8,128)(2,1)S(1)} %bitcast.2) | data formatting | bytes 1179648

commit v4 on v3

--- a/solution.py
+++ b/solution.py
@@ -10,7 +10,8 @@
 from jax.sharding import PartitionSpec as P
 
 MESH = pl.DeviceIdType.MESH
-CHUNKS = (((0, 1, 2, 3,4,5), 32), ((6, 7,8), 32))
+CHUNKS = (((0, 1), (0, 2)), ((1, 2), "01", "2"))
+MADE = {(0, 1): (1, 3), (0, 2): (2, 6), (1, 2): (5, 7), "01": (0, 4), "2": (8,)}
 
 
 def lag_table(freqs, blocks):
@@ -59,8 +60,8 @@
 
 
 def kernel(sizes, spectra_hbm, pair_slot_hbm, slot_cell_hbm, rank_hbm, table_hbm, out_ref, spectra_ref, pair_slot_ref,
-           slot_cell_ref, rank_ref, in_sems, mine, got, left, right_r,
-           right_i, slots, total, matches, table, send_a, recv_a, send_b, recv_b, table_sem,
+           slot_cell_ref, rank_ref, in_sems, mine, got, left, right, slots,
+           opposite, total, matches, table, send_a, recv_a, send_b, recv_b, table_sem,
            x_send, x_recv, a_send, a_recv, b_send, b_recv):
     groups, blocks, rows, cells = sizes
     sensors = blocks * rows
@@ -74,11 +75,17 @@
         copy.start()
     half = out_ref.shape[2] // blocks // 2
 
+    partners = [lax.rem(own_b + step, blocks) for step in sorted(range(1, blocks), key=lambda n: abs(n - blocks // 2))]
+    side = math.isqrt(groups)
+    hops = sorted(range(1, groups), key=lambda n: abs(n // side - side // 2) + abs(n % side - side // 2))
+    others_g = [
+        lax.rem(own_g // side + n // side, side) * side + lax.rem(lax.rem(own_g, side) + n % side, side) for n in hops
+    ]
     barrier = pltpu.get_barrier_semaphore()
-    for step in range(1, groups):
-        pl.semaphore_signal(barrier, inc=1, device_id=(lax.rem(own_g + step, groups), own_b), device_id_type=MESH)
-    for step in range(1, blocks):
-        pl.semaphore_signal(barrier, inc=1, device_id=(own_g, lax.rem(own_b + step, blocks)), device_id_type=MESH)
+    for to in partners:
+        pl.semaphore_signal(barrier, inc=1, device_id=(own_g, to), device_id_type=MESH)
+    for to in others_g:
+        pl.semaphore_signal(barrier, inc=1, device_id=(to, own_b), device_id_type=MESH)
     table_copy = pltpu.make_async_copy(table_hbm, table, table_sem)
     table_copy.start()
 
@@ -101,68 +108,142 @@
     matches[...] = one_hot(row_ids == at)
     pl.semaphore_wait(barrier, blocks + groups - 2)
 
-    def bins_copy(step):
-        to = lax.rem(own_b + step, blocks)
+    def bins_copy(to):
         return pltpu.make_async_remote_copy(
             src_ref=mine.at[to], dst_ref=got.at[own_b], send_sem=x_send, recv_sem=x_recv,
             device_id=(own_g, to), device_id_type=MESH)
 
-    for step in range(1, blocks):
-        bins_copy(step).start()
+    for to in partners:
+        bins_copy(to).start()
     got[own_b] = mine[own_b]
     others = got.at[pl.ds(0, blocks - 1)]
     wait_for(others, x_recv)
 
     low = lax.broadcasted_iota(jnp.int32, (sensors, 2 * half), 1) < half
+    wrap = right.shape[1] - sensors
+    plain, swapped = [], []
     for a in range(3):
         x = got[:, a].reshape(sensors, 2 * half).astype(jnp.float32)
-        swapped = pltpu.roll(x, half, 1)
+        plain.append(x)
+        swapped.append(pltpu.roll(x, half, 1))
+
+    def keep_right(n, x):
+        x = x.astype(jnp.bfloat16)
+        right[n, :sensors] = x
+        right[n, sensors:] = x[:wrap]
+
+    for a in range(3):
+        x, y = plain[a], swapped[a]
         left[a] = x
-        left[3 + a] = jnp.where(low, swapped, -swapped)
-        right_r[a] = jnp.where(low, x, swapped).astype(jnp.bfloat16)
-        right_i[a] = jnp.where(low, swapped, x).astype(jnp.bfloat16)
-    slots[...] = got[:, 3].reshape(sensors, sensors).astype(jnp.float32)
-
-    slot_count = total.shape[0]
+        left[3 + a] = jnp.where(low, y, -y)
+        if a > 0:
+            left[5 + a] = jnp.where(low, x, -x)
+            left[7 + a] = y
+        keep_right(a, jnp.where(low, x, y))
+        keep_right(3 + a, jnp.where(low, y, x))
+    real = jnp.where(low, plain[0], swapped[1])
+    imag = jnp.where(low, swapped[0], plain[1])
+    left[10] = real
+    left[11] = imag
+    keep_right(6, real)
+    keep_right(7, imag)
+
+    window = sensors // 2
+    table_of_slots = got[:, 3].reshape(sensors, sensors).astype(jnp.float32)
+    lane = lax.broadcasted_iota(jnp.int32, (window, sensors), 1)
+    pick = one_hot(lax.broadcasted_iota(jnp.int32, (sensors, rows * rows), 0)
+                   == window + lax.broadcasted_iota(jnp.int32, (sensors, rows * rows), 1) % rows)
+    keep = (lax.broadcasted_iota(jnp.int32, (window, rows * rows), 0) % rows
+            == lax.broadcasted_iota(jnp.int32, (window, rows * rows), 1) // rows)
+    for n, ordered in enumerate((table_of_slots, table_of_slots.T)):
+        turned = jnp.concatenate([
+            ordered[b * rows:(b + 1) * rows] if b == 0
+            else pltpu.roll(ordered[b * rows:(b + 1) * rows], sensors - b * rows, 1) for b in range(blocks)], axis=0)
+        joined = jnp.where(lane < window, turned[:window], pltpu.roll(turned[window:], window, 1))
+        if n == 1:
+            joined = jnp.where(lane % window < rows, -1.0, joined)
+        slots[n] = joined
+        spread = jnp.dot(turned[:window].astype(jnp.bfloat16), pick, preferred_element_type=jnp.float32)
+        spread = jnp.where(keep, spread, 0.0)
+        for b in range(blocks // 2):
+            line = jnp.sum(spread[b * rows:(b + 1) * rows], axis=0, keepdims=True)
+            for m in range(rows * rows // sensors):
+                opposite[n, m, b:b + 1] = line[:, m * sensors:(m + 1) * sensors]
+
+    slot_count = total.shape[1]
     slot_ids = lax.broadcasted_iota(jnp.int32, (slot_count, sensors), 0).astype(jnp.float32).astype(jnp.bfloat16)
 
-    def select(i):
-        row = jnp.broadcast_to(slots[pl.ds(i, 1), :], (16, sensors)).astype(jnp.bfloat16)
+    def select(row):
+        row = jnp.broadcast_to(row, (16, sensors)).astype(jnp.bfloat16)
         row = jnp.concatenate([row] * (slot_count // 16), axis=0)
         return jnp.where(row == slot_ids, jnp.bfloat16(1), jnp.bfloat16(0))
 
     def slot_sums(k):
-        chunk, per_step = CHUNKS[k]
-        width = spans[k][1]
+        chunk = CHUNKS[k]
+        width = 2 * half * len(chunk)
+
+        def factors(i, term, count):
+            def wide(n):
+                one = jnp.broadcast_to(left[n, pl.ds(i, 1), :], (16, 2 * half)).astype(jnp.bfloat16)
+                return jnp.concatenate([one] * (count // 16), axis=0) if count > 16 else one
+
+            if term == "01":
+                return wide(10), wide(11)
+            if term == "2":
+                return wide(2), wide(5)
+            a, b = term
+            return wide(a), wide(3 + a), wide(5 + b), wide(7 + b)
+
+        def products(i, at, count, term):
+            of = factors(i, term, count)
+            there = pl.ds(at, count)
+            if term == "01":
+                real, imag = right[6, there, :], right[7, there, :]
+                return of[0] * real + of[1] * imag, of[1] * real - of[0] * imag
+            if term == "2":
+                both = of[0] * right[2, there, :] + of[1] * right[5, there, :]
+                return both, both
+            a, b = term
+            one = of[0] * right[b, there, :] + of[1] * right[3 + b, there, :]
+            two = of[2] * right[a, there, :] + of[3] * right[3 + a, there, :]
+            return one + two, one - two
 
         def add(step, carried):
-            blocks_of = []
-            for u in range(per_step):
-                i = step * per_step + u
-                row = {}
-                for a in sorted({c // 3 for c in chunk}):
-                    for part in (a, 3 + a):
-                        wide = jnp.broadcast_to(left[part, pl.ds(i, 1), :], (16, 2 * half)).astype(jnp.bfloat16)
-                        row[part] = jnp.concatenate([wide] * (sensors // 16), axis=0)
-                terms = [row[c // 3] * right_r[c % 3] + row[3 + c // 3] * right_i[c % 3] for c in chunk]
-                blocks_of.append(jnp.concatenate(terms, axis=1))
-            products = jnp.concatenate(blocks_of, axis=0)
-            chosen = jnp.concatenate([select(step * per_step + u) for u in range(per_step)], axis=1)
-            total[:, :width] += jnp.dot(chosen, products, preferred_element_type=jnp.float32)
+            start = pl.multiple_of(step * rows, rows)
+            half_on = pl.multiple_of(step * rows + window, rows)
+            added, taken = [], []
+            pieces = [(start + u, start, window) for u in range(rows)], [(half_on + u, half_on, window) for u in range(rows)]
+            order = [piece for both in zip(*pieces) for piece in both]
+            order += [(start + u, half_on, rows) for u in range(rows)]
+            for i, at, count in order:
+                terms = [products(i, at, count, term) for term in chunk]
+                added.append(jnp.concatenate([t[0] for t in terms], axis=1))
+                taken.append(jnp.concatenate([t[1] for t in terms], axis=1))
+            sums, differences = [], []
+            for u in range(rows + rows * rows // sensors):
+                if u < rows:
+                    a, b = (select(slots[n, pl.ds(start + u, 1), :]) for n in range(2))
+                else:
+                    a, b = (select(opposite[n, u - rows, pl.ds(step, 1), :]) for n in range(2))
+                sums.append(a + b)
+                differences.append(a - b)
+            for n, (chosen, values) in enumerate(((sums, added), (differences, taken))):
+                total[n, :, :width] += jnp.dot(
+                    jnp.concatenate(chosen, axis=1), jnp.concatenate(values, axis=0), preferred_element_type=jnp.float32)
             return carried
 
-        total[:, :width] = jnp.zeros((slot_count, width), jnp.float32)
-        lax.fori_loop(0, sensors // per_step, add, 0)
-
+        total[:, :, :width] = jnp.zeros((2, slot_count, width), jnp.float32)
+        lax.fori_loop(0, blocks // 2, add, 0)
+
+    made = [tuple(c for term in chunk for c in MADE[term]) for chunk in CHUNKS]
     spans = []
-    first = 0
-    for chunk, _ in CHUNKS:
-        spans.append((first, 2 * half * len(chunk)))
-        first += 2 * half * len(chunk)
-
-    def sums_copy(k, step):
-        start, width = spans[k]
-        to = lax.rem(own_g + step, groups)
+    begin = 0
+    for pairs in made:
+        spans.append((begin, 2 * half * len(pairs)))
+        begin += 2 * half * len(pairs)
+
+    def sums_copy(k, to):
+        start, width = spans[k]
         return pltpu.make_async_remote_copy(
             src_ref=send_a.at[pl.ds(pl.multiple_of(to * share, share), share), pl.ds(start, width)],
             dst_ref=recv_a.at[pl.ds(pl.multiple_of(own_g * share, share), share), pl.ds(start, width)],
@@ -171,15 +252,29 @@
 
     def start_sums(k):
         start, width = spans[k]
-        send_a[:, start:start + width] = total[:, :width].astype(jnp.bfloat16)
-        for step in range(1, groups):
-            sums_copy(k, step).start()
+        first = lax.broadcasted_iota(jnp.int32, (slot_count, 2 * half), 1) < half
+        lines = []
+        for m, term in enumerate(CHUNKS[k]):
+            plus, minus = (total[n, :, 2 * half * m:2 * half * (m + 1)] for n in range(2))
+            if term == "2":
+                lines.append(jnp.where(first, plus, minus))
+            elif term == "01":
+                lines.append(jnp.where(first, plus, pltpu.roll(minus, half, 1)))
+                lines.append(jnp.where(first, pltpu.roll(plus, half, 1), minus))
+            else:
+                lines.append(0.5 * (plus + minus))
+                gap = 0.5 * (plus - minus)
+                lines.append(jnp.where(first, gap, -gap))
+        for m, line in enumerate(lines):
+            at = start + 2 * half * m
+            send_a[:, at:at + 2 * half] = line.astype(jnp.bfloat16)
+        for to in others_g:
+            sums_copy(k, to).start()
         own = pl.ds(pl.multiple_of(own_g * share, share), share)
         recv_a[own, start:start + width] = send_a[own, start:start + width]
 
-    def cells_copy(k, step):
-        start, width = spans[k]
-        to = lax.rem(own_b + step, blocks)
+    def cells_copy(k, to):
+        start, width = spans[k]
         return pltpu.make_async_remote_copy(
             src_ref=send_b.at[to, :, pl.ds(start, width)],
             dst_ref=recv_b.at[own_b, :, pl.ds(start, width)],
@@ -191,20 +286,20 @@
         wait_for(recv_a.at[pl.ds(0, (groups - 1) * share), pl.ds(start, width)], a_recv.at[k])
         stacked = jnp.dot(matches[...], recv_a[:, start:start + width], preferred_element_type=jnp.float32)
         send_b[:, :, start:start + width] = stacked.astype(jnp.bfloat16).reshape(blocks, cells, width)
-        for step in range(1, blocks):
-            cells_copy(k, step).start()
+        for to in partners:
+            cells_copy(k, to).start()
         recv_b[own_b, :, start:start + width] = send_b[own_b, :, start:start + width]
 
     def transform(k):
         start, width = spans[k]
         wait_for(recv_b.at[pl.ds(0, blocks - 1), :, pl.ds(start, width)], b_recv.at[k])
         lines = []
-        for m in range(len(CHUNKS[k][0])):
+        for m in range(len(made[k])):
             at = start + 2 * half * m
             lines.append(jnp.concatenate([recv_b[b, :, at:at + 2 * half] for b in range(blocks)], axis=1))
         spectrum = jnp.concatenate(lines, axis=0) if len(lines) > 1 else lines[0]
         lag = jnp.dot(spectrum, table[...], preferred_element_type=jnp.float32).astype(jnp.bfloat16)
-        for m, c in enumerate(CHUNKS[k][0]):
+        for m, c in enumerate(made[k]):
             out_ref[c] = lag[m * cells:(m + 1) * cells]
 
     count = len(CHUNKS)
@@ -241,7 +336,7 @@
 
     table = jnp.asarray(lag_table(freqs, blocks))
     count = len(CHUNKS)
-    widest = max(len(chunk) for chunk, _ in CHUNKS) * own_bins
+    widest = max(len(chunk) for chunk in CHUNKS) * own_bins
     vmem = pl.BlockSpec(memory_space=pltpu.VMEM)
     out = pl.pallas_call(
         functools.partial(kernel, (groups, blocks, rows, cells)),
@@ -256,11 +351,11 @@
             pltpu.SemaphoreType.DMA((4,)),
             pltpu.VMEM((blocks, 4, rows, own_bins), jnp.bfloat16),
             pltpu.VMEM((blocks, 4, rows, own_bins), jnp.bfloat16),
-            pltpu.VMEM((6, sensors, own_bins), jnp.float32),
-            pltpu.VMEM((3, sensors, own_bins), jnp.bfloat16),
-            pltpu.VMEM((3, sensors, own_bins), jnp.bfloat16),
-            pltpu.VMEM((sensors, sensors), jnp.float32),
-            pltpu.VMEM((slot_count, widest), jnp.float32),
+            pltpu.VMEM((12, sensors, own_bins), jnp.float32),
+            pltpu.VMEM((8, sensors + sensors // 2, own_bins), jnp.bfloat16),
+            pltpu.VMEM((2, sensors // 2, sensors), jnp.float32),
+            pltpu.VMEM((2, rows * rows // sensors, blocks, sensors), jnp.float32),
+            pltpu.VMEM((2, slot_count, widest), jnp.float32),
             pltpu.VMEM((blocks * cells, groups * share), jnp.bfloat16),
             pltpu.VMEM((2 * freqs, 2 * freqs), jnp.bfloat16),
             pltpu.VMEM((slot_count, width), jnp.bfloat16),

time: 37 us -> 35.1 us (0.949)
  Pallas kernels: 36.1 us -> 34.1 us
    pallas_call x1, Pallas kernels: 36.1 us -> 34.1 us  [on_device(): pl.pallas_call(functools.partial(kernel, (groups, blocks, rows, cells)),...]
where the time goes in v4:
time: 35.1 us; the launch traced here: 34.9 us
  Pallas kernels  34.1 us (97%)
  local copies, waits for them, and re-layouts  0.82 us (2%)
    pallas_call x1, Pallas kernels, on_device(): pl.pallas_call(functools.partial(kernel, (groups, blocks, rows, cells)),...  34.1 us
    unnamed x1, local copies, waits for them, and re-layouts  0.82 us

profile of v4, /device:TPU:1, one launch (start us, length us, event | category | flops | bytes accessed | tf_op | source)
XLA Modules:
  0.0 34.9 jit_solution(611863092843850315)
XLA Ops:
  0.0 34.1 %stack_pairs.1 = bf16[9,32,1024]{2,1,0:T(8,128)(2,1)S(1)} custom-call(bf16[16,3,2,512]{3,2,1,0:T(2,128)(2,1)} %spectra_hbm.1, s32[16,128]{1,0:T(8,128)} %pair_slot_hbm.1, s32[16,256]{1,0:T(8,128)} %slot_cell_hbm.1, s32[32,128]{1,0:T(8,128)} %bitcast.3, bf16[1024,1024]{1,0:T(8,128)(2,1)} %constant.2.clone.table_hbm), custom_call_target="tpu_custom_call" | custom-call | tf_op jit(solution)/shard_map/stack_pairs/pallas_call | solution.py:341
  34.1 0.8 %copy.7 = bf16[32,9,1024]{2,0,1:T(8,128)(2,1)} copy(bf16[32,9,1024]{2,0,1:T(8,128)(2,1)S(1)} %bitcast.2) | data formatting | bytes 1179648

commit v5 on v4

--- a/solution.py
+++ b/solution.py
@@ -10,7 +10,7 @@
 from jax.sharding import PartitionSpec as P
 
 MESH = pl.DeviceIdType.MESH
-CHUNKS = (((0, 1), (0, 2)), ((1, 2), "01", "2"))
+CHUNKS = (((0, 1), (0, 2)), ((1, 2), "01"), ("2",))
 MADE = {(0, 1): (1, 3), (0, 2): (2, 6), (1, 2): (5, 7), "01": (0, 4), "2": (8,)}
 
 
@@ -306,14 +306,12 @@
     for k in range(count):
         slot_sums(k)
         start_sums(k)
-        if k >= 1:
-            start_cells(k - 1)
     table_copy.wait()
-    for k in range(count - 2):
+    wait_for(others, x_send)
+    for k in range(count):
+        start_cells(k)
+    for k in range(count - 1):
         transform(k)
-    wait_for(others, x_send)
-    start_cells(count - 1)
-    transform(count - 2)
     for k in range(count):
         start, width = spans[k]
         wait_for(send_a.at[pl.ds(0, (groups - 1) * share), pl.ds(start, width)], a_send.at[k])

time: 35.1 us -> 33.6 us (0.957)
  Pallas kernels: 34.1 us -> 32.7 us
    pallas_call x1, Pallas kernels: 34.1 us -> 32.7 us  [on_device(): pl.pallas_call(functools.partial(kernel, (groups, blocks, rows, cells)),...]
where the time goes in v5:
time: 33.6 us; the launch traced here: 33.5 us
  Pallas kernels  32.7 us (97%)
  local copies, waits for them, and re-layouts  0.82 us (2%)
    pallas_call x1, Pallas kernels, on_device(): pl.pallas_call(functools.partial(kernel, (groups, blocks, rows, cells)),...  32.7 us
    unnamed x1, local copies, waits for them, and re-layouts  0.82 us

profile of v5, /device:TPU:1, one launch (start us, length us, event | category | flops | bytes accessed | tf_op | source)
XLA Modules:
  0.0 33.5 jit_solution(2036818229653532255)
XLA Ops:
  0.0 32.7 %stack_pairs.1 = bf16[9,32,1024]{2,1,0:T(8,128)(2,1)S(1)} custom-call(bf16[16,3,2,512]{3,2,1,0:T(2,128)(2,1)} %spectra_hbm.1, s32[16,128]{1,0:T(8,128)} %pair_slot_hbm.1, s32[16,256]{1,0:T(8,128)} %slot_cell_hbm.1, s32[32,128]{1,0:T(8,128)} %bitcast.3, bf16[1024,1024]{1,0:T(8,128)(2,1)} %constant.2.clone.table_hbm), custom_call_target="tpu_custom_call" | custom-call | tf_op jit(solution)/shard_map/stack_pairs/pallas_call | solution.py:339
  32.7 0.8 %copy.7 = bf16[32,9,1024]{2,0,1:T(8,128)(2,1)} copy(bf16[32,9,1024]{2,0,1:T(8,128)(2,1)S(1)} %bitcast.2) | data formatting | bytes 1179648

commit v6 on v5

--- a/solution.py
+++ b/solution.py
@@ -233,7 +233,7 @@
             return carried
 
         total[:, :, :width] = jnp.zeros((2, slot_count, width), jnp.float32)
-        lax.fori_loop(0, blocks // 2, add, 0)
+        lax.fori_loop(0, blocks // 2, add, 0, unroll=4)
 
     made = [tuple(c for term in chunk for c in MADE[term]) for chunk in CHUNKS]
     spans = []

time: 33.6 us -> 32 us (0.952)
  Pallas kernels: 32.7 us -> 31 us
    pallas_call x1, Pallas kernels: 32.7 us -> 31 us  [on_device(): pl.pallas_call(functools.partial(kernel, (groups, blocks, rows, cells)),...]
where the time goes in v6:
time: 32 us; the launch traced here: 31.8 us
  Pallas kernels  31 us (97%)
  local copies, waits for them, and re-layouts  0.82 us (3%)
    pallas_call x1, Pallas kernels, on_device(): pl.pallas_call(functools.partial(kernel, (groups, blocks, rows, cells)),...  31 us
    unnamed x1, local copies, waits for them, and re-layouts  0.82 us

profile of v6, /device:TPU:1, one launch (start us, length us, event | category | flops | bytes accessed | tf_op | source)
XLA Modules:
  0.0 31.8 jit_solution(4614422646616837048)
XLA Ops:
  0.0 31.0 %stack_pairs.1 = bf16[9,32,1024]{2,1,0:T(8,128)(2,1)S(1)} custom-call(bf16[16,3,2,512]{3,2,1,0:T(2,128)(2,1)} %spectra_hbm.1, s32[16,128]{1,0:T(8,128)} %pair_slot_hbm.1, s32[16,256]{1,0:T(8,128)} %slot_cell_hbm.1, s32[32,128]{1,0:T(8,128)} %bitcast.3, bf16[1024,1024]{1,0:T(8,128)(2,1)} %constant.2.clone.table_hbm), custom_call_target="tpu_custom_call" | custom-call | tf_op jit(solution)/shard_map/stack_pairs/pallas_call | solution.py:339
  31.0 0.8 %copy.7 = bf16[32,9,1024]{2,0,1:T(8,128)(2,1)} copy(bf16[32,9,1024]{2,0,1:T(8,128)(2,1)S(1)} %bitcast.2) | data formatting | bytes 1179648

commit v7 on v6

--- a/solution.py
+++ b/solution.py
@@ -308,18 +308,19 @@
         start_sums(k)
     table_copy.wait()
     wait_for(others, x_send)
+    start_cells(0)
+    start_cells(2)
+    start_cells(1)
+    transform(0)
+    transform(2)
     for k in range(count):
-        start_cells(k)
-    for k in range(count - 1):
-        transform(k)
-    for k in range(count):
         start, width = spans[k]
         wait_for(send_a.at[pl.ds(0, (groups - 1) * share), pl.ds(start, width)], a_send.at[k])
-        if k < count - 1:
+        if k != 1:
             wait_for(send_b.at[pl.ds(0, blocks - 1), :, pl.ds(start, width)], b_send.at[k])
-    transform(count - 1)
-    start, width = spans[count - 1]
-    wait_for(send_b.at[pl.ds(0, blocks - 1), :, pl.ds(start, width)], b_send.at[count - 1])
+    transform(1)
+    start, width = spans[1]
+    wait_for(send_b.at[pl.ds(0, blocks - 1), :, pl.ds(start, width)], b_send.at[1])
 
 
 def on_device(spectra, pair_slot, slot_cell, cell_rank):

time: 32 us -> 31.6 us (0.988)
    pallas_call x1, Pallas kernels: 31 us -> 30.7 us  [on_device(): pl.pallas_call(functools.partial(kernel, (groups, blocks, rows, cells)),...]
where the time goes in v7:
time: 31.6 us; the launch traced here: 31.5 us
  Pallas kernels  30.7 us (97%)
  local copies, waits for them, and re-layouts  0.82 us (3%)
    pallas_call x1, Pallas kernels, on_device(): pl.pallas_call(functools.partial(kernel, (groups, blocks, rows, cells)),...  30.7 us
    unnamed x1, local copies, waits for them, and re-layouts  0.82 us

profile of v7, /device:TPU:1, one launch (start us, length us, event | category | flops | bytes accessed | tf_op | source)
XLA Modules:
  0.0 31.5 jit_solution(2244076653224603477)
XLA Ops:
  0.0 30.7 %stack_pairs.1 = bf16[9,32,1024]{2,1,0:T(8,128)(2,1)S(1)} custom-call(bf16[16,3,2,512]{3,2,1,0:T(2,128)(2,1)} %spectra_hbm.1, s32[16,128]{1,0:T(8,128)} %pair_slot_hbm.1, s32[16,256]{1,0:T(8,128)} %slot_cell_hbm.1, s32[32,128]{1,0:T(8,128)} %bitcast.3, bf16[1024,1024]{1,0:T(8,128)(2,1)} %constant.2.clone.table_hbm), custom_call_target="tpu_custom_call" | custom-call | tf_op jit(solution)/shard_map/stack_pairs/pallas_call | solution.py:340
  30.7 0.8 %copy.7 = bf16[32,9,1024]{2,0,1:T(8,128)(2,1)} copy(bf16[32,9,1024]{2,0,1:T(8,128)(2,1)S(1)} %bitcast.2) | data formatting | bytes 1179648
